TPU v7x, 256 devices: a whole 4x4x8 slice. The times are simulated.
256 devices in a mesh: section: 16 (over y_hi, x, core), tensor: 16 (over y_lo, z).
Axes of the slice: x: 4, y: 4 (y_hi: 2, y_lo: 2; y = y_hi * 2 + y_lo), z: 8, core: 2. Of those that a mesh axis runs over, the one named last changes fastest.
Arguments:
- x_saved: bfloat16 [16, 2, 256, 4608], P('section', None, None, 'tensor'), may hold values from -12 to 12
- grad_first: bfloat16 [16, 256, 4608], P('section', None, 'tensor'), may hold values from -6 to 6
- gains: float32 [32, 4608], replicated, may hold values from 0.1 to 1.9
- assign: int32 [16, 2], P('section'), may hold values from 0 to 31
- order: int32 [16], replicated, may hold values from 0 to 1
- w_query: bfloat16 [4608, 4096], P(None, 'tensor'), may hold values from -0.088388348 to 0.088388348
- w_key: bfloat16 [4608, 2048], P(None, 'tensor'), may hold values from -0.088388348 to 0.088388348
- w_value: bfloat16 [4608, 2048], P(None, 'tensor'), may hold values from -0.09375 to 0.09375
- w_output: bfloat16 [4096, 4608], P('tensor'), may hold values from -0.09375 to 0.09375
Outputs:
- input_grad: bfloat16 [16, 256, 4608], P('section', None, 'tensor')
- grad_query: float32 [4608, 4096], P('section', 'tensor')
- grad_key: float32 [4608, 2048], P('section', 'tensor')
- grad_value: float32 [4608, 2048], P('section', 'tensor')
- grad_output: float32 [4096, 4608], P('tensor', 'section')
All inputs are finite; a program needn't handle non-finite values.
Results may differ from a plain program's by a relative error of at most 0.033.
Values may be sent and summed in bfloat16 or wider, within the bound.
No kernel may reach another device: no remote copies, remote signals or barrier semaphores. Data moves between devices by JAX's collectives and lax.ppermute only.
A program may use at most 128 MiB of HBM per device.

v0:
```python
import jax
import jax.numpy as jnp
from jax import lax
from jax.sharding import PartitionSpec as P

HD = 128


def shifted(shard, axis, by):
    length = lax.axis_size(axis)
    return lax.ppermute(shard, axis, [(i, (i + by) % length) for i in range(length)])


def local_attention(scaled, upstream, w_query, w_key, w_value, w_output):
    f32 = jnp.float32
    tokens = scaled.shape[0]
    local_heads = w_query.shape[1] // HD
    local_kv = w_key.shape[1] // HD
    group = local_heads // local_kv
    factor = HD ** (-0.5)
    query = (
        jnp.dot(scaled, w_query, preferred_element_type=f32)
        .astype(jnp.bfloat16)
        .reshape(tokens, local_heads, HD)
    )
    keys = (
        jnp.dot(scaled, w_key, preferred_element_type=f32)
        .astype(jnp.bfloat16)
        .reshape(tokens, local_kv, HD)
    )
    values = (
        jnp.dot(scaled, w_value, preferred_element_type=f32)
        .astype(jnp.bfloat16)
        .reshape(tokens, local_kv, HD)
    )
    keys_rep = jnp.repeat(keys, group, axis=1)
    values_rep = jnp.repeat(values, group, axis=1)
    scores = jnp.einsum("thd,uhd->htu", query, keys_rep, preferred_element_type=f32) * factor
    rows = lax.broadcasted_iota(jnp.int32, (tokens, tokens), 0)
    cols = lax.broadcasted_iota(jnp.int32, (tokens, tokens), 1)
    causal = (cols <= rows)[None]
    scores = jnp.where(causal, scores, -1e30)
    top = jnp.max(scores, axis=-1, keepdims=True)
    expo = jnp.where(causal, jnp.exp(scores - top), 0.0)
    probs = expo / jnp.sum(expo, axis=-1, keepdims=True)
    probs_b = probs.astype(jnp.bfloat16)
    attended = jnp.einsum("htu,uhd->thd", probs_b, values_rep, preferred_element_type=f32).astype(
        jnp.bfloat16
    )
    attended = attended.reshape(tokens, local_heads * HD)
    grad_att = jnp.einsum("td,cd->tc", upstream, w_output, preferred_element_type=f32).astype(
        jnp.bfloat16
    )
    grad_heads = grad_att.reshape(tokens, local_heads, HD)
    grad_probs = jnp.einsum("thd,uhd->htu", grad_heads, values_rep, preferred_element_type=f32)
    delta = jnp.sum(probs * grad_probs, axis=-1, keepdims=True)
    grad_scores = (probs * (grad_probs - delta) * factor).astype(jnp.bfloat16)
    grad_query = jnp.einsum(
        "htu,uhd->thd", grad_scores, keys_rep, preferred_element_type=f32
    ).astype(jnp.bfloat16)
    grad_key_full = jnp.einsum("htu,thd->uhd", grad_scores, query, preferred_element_type=f32)
    grad_key = grad_key_full.reshape(tokens, local_kv, group, HD).sum(axis=2).astype(jnp.bfloat16)
    grad_val_full = jnp.einsum("htu,thd->uhd", probs_b, grad_heads, preferred_element_type=f32)
    grad_value = grad_val_full.reshape(tokens, local_kv, group, HD).sum(axis=2).astype(jnp.bfloat16)
    grad_query = grad_query.reshape(tokens, local_heads * HD)
    grad_key = grad_key.reshape(tokens, local_kv * HD)
    grad_value = grad_value.reshape(tokens, local_kv * HD)
    branch = (
        jnp.einsum("tc,dc->td", grad_query, w_query, preferred_element_type=f32)
        + jnp.einsum("tc,dc->td", grad_key, w_key, preferred_element_type=f32)
        + jnp.einsum("tc,dc->td", grad_value, w_value, preferred_element_type=f32)
    )
    projected = jnp.concatenate([grad_query, grad_key, grad_value], axis=1)
    return (branch, projected, attended)


def pick_value(table, position):
    places = lax.iota(jnp.int32, table.shape[0])
    return jnp.sum(jnp.where(places == position, table, 0))


def pick_row(table, position):
    places = lax.iota(jnp.int32, table.shape[0])
    return jnp.sum(jnp.where((places == position)[:, None], table, 0.0), axis=0)


def body(x_saved, grad_first, gains, assign, order, w_query, w_key, w_value, w_output):
    f32 = jnp.float32
    section_count = lax.axis_size("section")
    section_pos = lax.axis_index("section")
    tensor_pos = lax.axis_index("tensor")
    width = x_saved.shape[3]
    own_batch = pick_value(order, section_pos)
    next_batch = pick_value(order, (section_pos + 1) % section_count)
    first_scale = pick_row(gains, assign[0, 0])
    second_scale = pick_row(gains, assign[0, 1])
    first_share = lax.dynamic_slice_in_dim(first_scale, tensor_pos * width, width)
    second_share = lax.dynamic_slice_in_dim(second_scale, tensor_pos * width, width)
    first_input = jnp.where(own_batch == 0, x_saved[0, 0], x_saved[0, 1])
    second_input = jnp.where(next_batch == 0, x_saved[0, 0], x_saved[0, 1])
    first_scaled = (first_input.astype(f32) * first_share).astype(jnp.bfloat16)
    second_scaled = (second_input.astype(f32) * second_share).astype(jnp.bfloat16)
    first_rows, second_rows, first_grad = (
        lax.all_gather(first_scaled, "tensor", axis=1, tiled=True),
        lax.all_gather(second_scaled, "tensor", axis=1, tiled=True),
        lax.all_gather(grad_first[0], "tensor", axis=1, tiled=True),
    )
    first_branch, first_proj, first_att = local_attention(
        first_rows, first_grad, w_query, w_key, w_value, w_output
    )
    branch_part = lax.psum_scatter(
        first_branch.astype(jnp.bfloat16), "tensor", scatter_dimension=1, tiled=True
    ).astype(jnp.float32)
    first_dx = (grad_first[0].astype(f32) + first_share * branch_part).astype(jnp.bfloat16)
    second_piece = shifted(first_dx, "section", -1)
    second_grad = lax.all_gather(second_piece, "tensor", axis=1, tiled=True)
    second_branch, second_proj, second_att = local_attention(
        second_rows, second_grad, w_query, w_key, w_value, w_output
    )
    second_part = lax.psum_scatter(
        second_branch.astype(jnp.bfloat16), "tensor", scatter_dimension=1, tiled=True
    ).astype(jnp.float32)
    second_dx = (second_piece.astype(f32) + second_share * second_part).astype(jnp.bfloat16)
    both_rows = jnp.concatenate([first_rows, second_rows], axis=0)
    both_grads = jnp.concatenate([first_grad, second_grad], axis=0)
    both_proj = jnp.concatenate([first_proj, second_proj], axis=0)
    both_att = jnp.concatenate([first_att, second_att], axis=0)
    left = jnp.einsum("tr,tc->rc", both_rows, both_proj, preferred_element_type=f32)
    right = jnp.einsum("tr,tc->rc", both_grads, both_att, preferred_element_type=f32)
    shared = lax.psum_scatter(
        jnp.concatenate([left, right], axis=1).astype(jnp.bfloat16),
        "section",
        scatter_dimension=0,
        tiled=True,
    ).astype(jnp.float32)
    query_cols = w_query.shape[1]
    key_cols = w_key.shape[1]
    grad_query = shared[:, :query_cols]
    grad_key = shared[:, query_cols : query_cols + key_cols]
    grad_value = shared[:, query_cols + key_cols : query_cols + 2 * key_cols]
    grad_output = shared[:, query_cols + 2 * key_cols :].T
    return (second_dx[None], grad_query, grad_key, grad_value, grad_output)


def solution(mesh):
    in_specs = (
        P("section", None, None, "tensor"),
        P("section", None, "tensor"),
        P(),
        P("section", None),
        P(),
        P(None, "tensor"),
        P(None, "tensor"),
        P(None, "tensor"),
        P("tensor", None),
    )
    out_specs = (
        P("section", None, "tensor"),
        P("section", "tensor"),
        P("section", "tensor"),
        P("section", "tensor"),
        P("tensor", "section"),
    )
    return jax.shard_map(body, mesh=mesh, in_specs=in_specs, out_specs=out_specs, check_vma=False)
```

profile of v0, /device:TPU:8, one launch (start us, length us, event | category | flops | bytes accessed | tf_op | source)
XLA Modules:
  0.0 597.1 jit_solution(840008831195591815)
XLA Ops:
  7.2 1.4 fusion.81
  10.0 1.3 fusion.120
  11.3 1.3 iota_compare_fusion.1
  12.6 1.3 select_reduce_fusion
  14.1 1.9 fusion.51
  16.1 0.7 all-gather.12.cloned.1.call-update
  16.8 0.6 iota_compare_fusion
  17.5 72.9 %all-gather.6.cloned.1.call-done = bf16[256,4608]{0,1:T(8,128)(2,1)} async-done(((bf16[256,288]{0,1:T(8,128)(2,1)}), bf16[256,4608]{0,1:T(8,128)(2,1)}) %all-gather.6.cloned.1.call-update) | async-done | bytes 2359312 | tf_op jit(solution)/shard_map/all_gather | solution.py:104
  90.4 3.4 convolution_convert_fusion.13
  93.8 1.6 copy.38
  95.4 3.1 convolution_convert_fusion.12
  98.5 0.9 copy.41
  99.4 62.5 %all-gather.12.cloned.1.call-done = bf16[1,256,4608]{1,2,0:T(8,128)(2,1)} async-done(((bf16[1,256,288]{1,2,0:T(8,128)(2,1)}), bf16[1,256,4608]{1,2,0:T(8,128)(2,1)}) %all-gather.12.cloned.1.call-update) | async-done | bytes 2359312 | tf_op jit(solution)/shard_map/all_gather | solution.py:106
  161.9 3.3 convolution_convert_fusion.3
  165.2 0.3 fusion.72
  165.5 1.1 convolution_convert_fusion.9
  166.7 1.2 fusion.121
  167.9 2.2 convolution_convert_fusion.8
  170.1 2.2 fusion.28
  172.2 1.2 fusion.29
  173.5 1.8 fusion.127
  175.3 0.8 convolution_add_fusion.3
  176.1 0.5 copy-done.4
  176.6 2.2 fusion.4
  178.8 0.5 all-gather.8.cloned.1.call-update
  179.4 71.9 %reduce-scatter.6.cloned.1.call-done = bf16[256,288]{0,1:T(8,128)(2,1)} async-done(((bf16[256,4608]{0,1:T(8,128)(2,1)}), bf16[256,288]{0,1:T(8,128)(2,1)}) %reduce-scatter.6.cloned.1.call-update) | async-done | bytes 147472 | tf_op jit(solution)/shard_map/reduce_scatter | solution.py:111
  251.3 1.1 fusion.53
  252.4 0.1 collective-permute-start
  252.5 2.7 collective-permute-done
  255.2 0.2 reduce-scatter.8.cloned.1.call-start
  255.4 66.4 %all-gather.8.cloned.1.call-done = bf16[256,4608]{0,1:T(8,128)(2,1)} async-done(((bf16[256,288]{0,1:T(8,128)(2,1)}), bf16[256,4608]{0,1:T(8,128)(2,1)}) %all-gather.8.cloned.1.call-update) | async-done | bytes 2359312 | tf_op jit(solution)/shard_map/all_gather | solution.py:105
  321.8 3.4 convolution_convert_fusion.10
  325.3 1.6 copy.50
  326.8 3.1 convolution_convert_fusion.11
  329.9 1.6 copy.47
  331.5 3.4 convolution_convert_fusion.7
  334.9 2.2 fusion.124
  337.0 56.2 %all-gather.10.cloned.1.call-done = bf16[256,4608]{0,1:T(8,128)(2,1)} async-done(((bf16[256,288]{0,1:T(8,128)(2,1)}), bf16[256,4608]{0,1:T(8,128)(2,1)}) %all-gather.10.cloned.1.call-update) | async-done | bytes 2359312 | tf_op jit(solution)/shard_map/all_gather | solution.py:116
  393.2 3.2 convolution_convert_fusion.2
  396.4 1.1 fusion.67
  397.5 2.3 fusion.31
  399.8 2.5 fusion.30
  402.3 2.5 convolution_convert_fusion.6
  404.8 1.7 fusion.128
  406.5 0.8 convolution_add_fusion.1
  407.3 0.5 copy-done.5
  407.8 2.2 fusion.5
  410.0 0.7 copy-done.10
  410.8 0.1 copy-done.29
  410.9 1.5 convolution_convert_fusion.5
  412.4 1.5 convolution_convert_fusion.4
  414.0 4.0 convolution_convert_fusion.1
  418.1 4.3 convolution_convert_fusion
  422.4 5.7 pad_maximum_fusion
  428.1 10.3 %copy.78 = bf16[4608,768]{1,0:T(8,128)(2,1)} copy(bf16[4608,768]{0,1:T(8,128)(2,1)} %pad_maximum_fusion) | data formatting | bytes 14155776
  438.4 44.1 %reduce-scatter.8.cloned.1.call-done = bf16[256,288]{0,1:T(8,128)(2,1)} async-done(((bf16[256,4608]{0,1:T(8,128)(2,1)}), bf16[256,288]{0,1:T(8,128)(2,1)}) %reduce-scatter.8.cloned.1.call-update) | async-done | bytes 147472 | tf_op jit(solution)/shard_map/reduce_scatter | solution.py:120
  482.5 1.8 fusion.61
  484.3 99.6 %reduce-scatter.10.cloned.1.call-done = bf16[288,768]{1,0:T(8,128)(2,1)} async-done(((bf16[4608,768]{1,0:T(8,128)(2,1)}), bf16[288,768]{1,0:T(8,128)(2,1)}) %reduce-scatter.10.cloned.1.call-update) | async-done | bytes 442384
  583.9 1.3 copy.79
  585.3 0.7 fusion.119
  586.1 0.9 copy.61
  586.9 0.9 copy.58
  587.8 1.7 copy.59
  589.5 0.8 copy.60
  (74 shorter events, 0.8 us)
Async XLA Ops:
  7.2 158.3 %copy-start = (bf16[4608,256]{1,0:T(8,128)(2,1)S(1)}, bf16[4608,256]{1,0:T(8,128)(2,1)}, u32[]{:S(2)}) copy-start(bf16[4608,256]{1,0:T(8,128)(2,1)} %param.14) | copy-start | bytes 7077892
  7.2 83.2 %all-gather.6.cloned.1.call-start = ((), (), s32[]{:S(2)}) async-start(), calls=%async_computation.3 | async-start | bytes 2506752 | tf_op jit(solution)/shard_map/all_gather | solution.py:104
  13.9 81.5 %copy-start.3 = (bf16[4608,128]{1,0:T(8,128)(2,1)S(1)}, bf16[4608,128]{1,0:T(8,128)(2,1)}, u32[]{:S(2)}) copy-start(bf16[4608,128]{1,0:T(8,128)(2,1)} %param.16) | copy-start | bytes 3538948
  16.0 145.9 %all-gather.12.cloned.1.call-start = ((), (), s32[]{:S(2)}) async-start(), calls=%async_computation.8 | async-start | bytes 2506752 | tf_op jit(solution)/shard_map/all_gather | solution.py:106
  16.8 234.5 %reduce-scatter.6.cloned.1.call-start = ((), (), s32[]{:S(2)}) async-start(), calls=%async_computation.4 | async-start | bytes 2506752 | tf_op jit(solution)/shard_map/reduce_scatter | solution.py:111
  99.4 65.8 %copy-start.9 = (bf16[256,128]{0,1:T(8,128)(2,1)}, bf16[256,128]{0,1:T(8,128)(2,1)S(1)}, u32[]{:S(2)}) copy-start(bf16[256,128]{0,1:T(8,128)(2,1)S(1)} %copy.41) | copy-start | bytes 196612
  161.9 3.6 copy-start.6
  165.5 1.1 copy-start.24
  165.5 1.1 copy-start.25
  166.6 5.6 copy-start.28
  173.5 1.8 copy-start.2
  173.5 1.8 copy-start.16
  175.3 1.3 copy-start.4
  175.3 1.3 copy-start.18
  178.8 143.0 %all-gather.8.cloned.1.call-start = ((), (), s32[]{:S(2)}) async-start(), calls=%async_computation.5 | async-start | bytes 2506752 | tf_op jit(solution)/shard_map/all_gather | solution.py:105
  179.4 213.8 %all-gather.10.cloned.1.call-start = ((), (), s32[]{:S(2)}) async-start(), calls=%async_computation.6 | async-start | bytes 2506752 | tf_op jit(solution)/shard_map/all_gather | solution.py:116
  252.4 2.8 collective-permute-start
  255.2 227.4 %reduce-scatter.8.cloned.1.call-start = ((), (), s32[]{:S(2)}) async-start(), calls=%async_computation.7 | async-start | bytes 2506752 | tf_op jit(solution)/shard_map/reduce_scatter | solution.py:120
  393.2 3.2 copy-start.11
  396.4 1.1 copy-start.15
  404.8 1.7 copy-start.22
  406.5 1.3 copy-start.5
  406.5 1.3 copy-start.20
  409.9 0.8 copy-start.10
  409.9 0.9 copy-start.26
  409.9 1.0 copy-start.29
  409.9 2.5 copy-start.12
  409.9 2.5 copy-start.27
  410.0 2.5 copy-start.30
  410.0 173.9 %reduce-scatter.10.cloned.1.call-start = ((), (), s32[]{:S(2)}) async-start(), calls=%async_computation.9 | async-start | bytes 7520256
  413.9 4.0 copy-start.7
  414.0 4.0 copy-start.8
  414.0 4.0 copy-start.13
  414.0 4.0 copy-start.14
  414.0 4.0 copy-start.17
  414.0 4.0 copy-start.19
  414.0 4.0 copy-start.21
  414.0 4.0 copy-start.23
  585.2 5.0 copy-start.1
Sparse Core Ops, SparseCore 0:
  16.1 74.1 all-gather.5
  92.2 69.6 all-gather.11
  178.9 72.3 reduce-scatter.5
  253.5 68.2 all-gather.7
  323.5 69.7 all-gather.9
  410.1 72.3 reduce-scatter.7
  487.0 96.7 reduce-scatter.9
where the time goes:
time: 599 us; the launch traced here: 597 us
  waiting for transfers between devices  478 us (80%)
  matrix products  62.2 us (10%)
  local copies, waits for them, and re-layouts  25.6 us (4%)
  between operations  15.9 us (3%)
  other arithmetic  15.2 us (3%)
    unnamed x8, waiting for transfers between devices  101 us
    all_gather x1, waiting for transfers between devices, body(): lax.all_gather(first_scaled, 'tensor', axis=1, tiled=True)  72.9 us
    reduce_scatter x1, waiting for transfers between devices, body(): lax.psum_scatter(first_branch.astype(jnp.bfloat16), 'tensor', scatter_dim...  71.9 us
    all_gather x1, waiting for transfers between devices, body(): lax.all_gather(second_scaled, 'tensor', axis=1, tiled=True)  66.4 us
    all_gather x1, waiting for transfers between devices, body(): lax.all_gather(grad_first[0], 'tensor', axis=1, tiled=True)  62.5 us
    all_gather x1, waiting for transfers between devices, body(): second_grad = lax.all_gather(second_piece, 'tensor', axis=1, tiled=True)  56.2 us
    reduce_scatter x1, waiting for transfers between devices, body(): lax.psum_scatter(second_branch.astype(jnp.bfloat16), 'tensor', scatter_di...  44.1 us
    unnamed x68, local copies, waits for them, and re-layouts  17.7 us
  transfers between devices with their start and end apart: 8, of which 8 were waited for; matrix products, arithmetic and copies ran while one was open for 9% of the time, Pallas kernels for 0%

commit v1 on v0

v1 whole, which is shorter than its diff:
```python
import functools

import jax
import jax.numpy as jnp
from jax import lax
from jax.experimental import pallas as pl
from jax.experimental.pallas import tpu as pltpu
from jax.sharding import PartitionSpec as P

HD = 128
F32 = jnp.float32
BF16 = jnp.bfloat16
ROW = (((1,), (0,)), ((), ()))
NT = (((1,), (1,)), ((), ()))
TN = (((0,), (0,)), ((), ()))


def mul(a, b, dims):
    return lax.dot_general(a, b, dims, preferred_element_type=F32)


def along_z(by):
    return [(t, (t & 8) | ((t + by) & 7)) for t in range(16)]


def along_x(by):
    return [(s, (s & 9) | ((((s >> 1) + by) & 3) << 1)) for s in range(16)]


SWAP_Y = [(t, t ^ 8) for t in range(16)]
SWAP_CORE = [(s, s ^ 1) for s in range(16)]
SWAP_YHI = [(s, s ^ 8) for s in range(16)]


def to_previous(flip):
    pairs = []
    for s in range(16):
        for t in range(16):
            pairs.append((s * 16 + t, ((s - 1) % 16) * 16 + (t ^ flip)))
    return pairs


def send(a, axis, pairs):
    return lax.ppermute(a, axis, pairs)


def ring(payload):
    up, down = payload, payload
    found = {0: payload}
    for step in (1, 2, 3):
        up = send(up, "tensor", along_z(1))
        down = send(down, "tensor", along_z(-1))
        found[-step] = up
        found[step] = down
    far = (
        send(up[:, :144], "tensor", along_z(1)),
        send(down[:, 144:], "tensor", along_z(-1)),
    )
    return found, far


def assemble_kernel(routes, inputs, place_ref, *refs):
    ins, outs, sems = refs[:inputs], refs[inputs:-1], refs[-1]
    copies = []
    for number, (source, row, target, plane, offset, half) in enumerate(routes):
        depth = (place_ref[1] + offset) % 8
        if plane is None:
            dst = outs[target].at[depth]
        else:
            level = (place_ref[0] + plane) % 2 if plane < 2 else plane - 2
            dst = outs[target].at[level, depth]
        if half is not None:
            dst = dst.at[pl.ds(half * 144, 144)]
        copy = pltpu.make_async_copy(ins[source].at[row], dst, sems.at[number])
        copy.start()
        copies.append(copy)
    for copy in copies:
        copy.wait()


def assemble(arrays, routes, out_shapes, place):
    any_space = pl.BlockSpec(memory_space=pl.ANY)
    return pl.pallas_call(
        functools.partial(assemble_kernel, routes, len(arrays)),
        out_shape=[jax.ShapeDtypeStruct(shape, BF16) for shape in out_shapes],
        in_specs=[pl.BlockSpec(memory_space=pltpu.SMEM)] + [any_space] * len(arrays),
        out_specs=[any_space] * len(out_shapes),
        scratch_shapes=[pltpu.SemaphoreType.DMA((len(routes),))],
        cost_estimate=pl.CostEstimate(flops=0, bytes_accessed=5000000, transcendentals=0),
    )(place, *arrays)


class Routes:
    def __init__(self):
        self.arrays, self.routes = [], []

    def add(self, array, pieces):
        at = len(self.arrays)
        self.arrays.append(array)
        for row, (target, plane, offset, half) in enumerate(pieces):
            self.routes.append((at, row, target, plane, offset, half))


def scatter_chain(parts, plane, z):
    def part(offset):
        place = (z + offset) % 8
        return lax.dynamic_slice(parts, (plane, place, 0, 0), (1, 1, 288, 256))[0, 0]

    far = part(4)
    up = send(far[:144], "tensor", along_z(1))
    down = send(far[144:], "tensor", along_z(-1))
    near = part(3)
    up = jnp.concatenate([near[:144] + up, near[144:]], axis=0)
    near = part(-3)
    down = jnp.concatenate([near[:144], near[144:] + down], axis=0)
    for step in (2, 1, 0):
        up = send(up, "tensor", along_z(1))
        down = send(down, "tensor", along_z(-1))
        if step:
            up = part(step) + up
            down = part(-step) + down
    return part(0).astype(F32) + up.astype(F32) + down.astype(F32)


def section_scatter(mine, core, x, yhi):
    columns = mine.shape[-1]

    def side(which):
        return lax.dynamic_slice(mine, (0, 0, which, 0, 0), (2, 4, 1, 288, columns))[:, :, 0]

    both = side(core) + send(side(1 - core), "section", SWAP_CORE)

    def part(offset):
        return lax.dynamic_slice(both, (0, (x + offset) % 4, 0, 0), (2, 1, 288, columns))[:, 0]

    far = part(2)
    up = send(far[:1], "section", along_x(1))
    down = send(far[1:], "section", along_x(-1))
    near = part(1)
    up = jnp.concatenate([near[:1] + up, near[1:]], axis=0)
    near = part(-1)
    down = jnp.concatenate([near[:1], near[1:] + down], axis=0)
    up = send(up, "section", along_x(1))
    down = send(down, "section", along_x(-1))
    total = part(0).astype(F32) + up.astype(F32) + down.astype(F32)
    away = lax.dynamic_slice(total, (1 - yhi, 0, 0), (1, 288, columns))[0].astype(BF16)
    keep = lax.dynamic_slice(total, (yhi, 0, 0), (1, 288, columns))[0]
    return keep + send(away, "section", SWAP_YHI).astype(F32)


def forward(n, weights):
    proj = mul(weights, n, TN).astype(BF16)
    q, k, v = proj[:256], proj[256:384], proj[384:]
    j = lax.broadcasted_iota(jnp.int32, (256, 256), 0)
    i = lax.broadcasted_iota(jnp.int32, (256, 256), 1)
    causal = j <= i
    probs, outs = [], []
    for h in range(2):
        scores = mul(k, q[h * HD : (h + 1) * HD], TN) * (HD**-0.5)
        scores = jnp.where(causal, scores, -1e30)
        top = jnp.max(scores, axis=0, keepdims=True)
        expo = jnp.where(causal, jnp.exp(scores - top), 0.0)
        p = expo / jnp.sum(expo, axis=0, keepdims=True)
        probs.append(p)
        outs.append(mul(v, p.astype(BF16), ROW).astype(BF16))
    return q, k, v, probs, jnp.concatenate(outs, axis=0)


def backward(saved, g, w_output):
    q, k, v, probs, _ = saved
    d_o = mul(w_output, g, ROW).astype(BF16)
    d_q, d_k, d_v = [], 0.0, 0.0
    for h in range(2):
        d_oh = d_o[h * HD : (h + 1) * HD]
        p = probs[h]
        dp = mul(v, d_oh, TN)
        delta = jnp.sum(p * dp, axis=0, keepdims=True)
        ds = (p * (dp - delta) * (HD**-0.5)).astype(BF16)
        d_q.append(mul(k, ds, ROW).astype(BF16))
        d_k = d_k + mul(q[h * HD : (h + 1) * HD], ds, NT)
        d_v = d_v + mul(d_oh, p.astype(BF16), NT)
    return jnp.concatenate(d_q + [d_k.astype(BF16), d_v.astype(BF16)], axis=0)


def body(x_saved, grad_first, gains, assign, order, w_query, w_key, w_value, w_output):
    s = lax.axis_index("section")
    t = lax.axis_index("tensor")
    z, y = t % 8, t // 8
    core, x, yhi = s % 2, (s // 2) % 4, s // 8
    place = jnp.stack([y, z]).astype(jnp.int32)
    shares = gains.reshape(32, 16, 288)
    previous = [(i, (i - 1) % 16) for i in range(16)]

    def share(which, shard):
        return lax.dynamic_slice(shares, (which, shard, 0), (1, 1, 288)).reshape(288, 1)

    first_share = share(assign[0, 0], t)
    second_share = share(assign[0, 1], t)
    own_batch = lax.dynamic_slice(order, (s,), (1,))[0]
    next_batch = lax.dynamic_slice(order, ((s + 1) % 16,), (1,))[0]

    def scaled(batch, scale):
        rows = jnp.where(batch == 0, x_saved[0, 0], x_saved[0, 1])
        return (rows.T.astype(F32) * scale).astype(BF16)

    full = (2, 8, 288, 256)
    plane = (8, 288, 256)

    own = jnp.stack([scaled(own_batch, first_share), grad_first[0].T])
    other = send(own, "tensor", SWAP_Y)
    found, far = ring(own)
    found_n, far_n = ring(other[:1])
    routes = Routes()
    for offset, block in found.items():
        routes.add(block, [(0, 0, offset, None), (1, 0, offset, None)])
    for half in (0, 1):
        routes.add(far[half], [(0, 0, 4, half), (1, 0, 4, half)])
    for offset, block in found_n.items():
        if offset:
            routes.add(block, [(0, 1, offset, None)])
    for half in (0, 1):
        routes.add(far_n[half], [(0, 1, 4, half)])
    routes.add(other, [(0, 1, 0, None), (1, 1, 0, None)])
    for step in (1, 2, 3):
        swapped = send(jnp.stack([found[step][1], found[-step][1]]), "tensor", SWAP_Y)
        routes.add(swapped, [(1, 1, step, None), (1, 1, -step, None)])
    swapped = send(jnp.stack([far[0][1], far[1][1]]), "tensor", SWAP_Y)
    routes.add(swapped, [(1, 1, 4, 0), (1, 1, 4, 1)])
    n1_full, g1_full = assemble(routes.arrays, routes.routes, [full, full], place)
    n1_full = n1_full.reshape(4608, 256)
    g1_full = g1_full.reshape(4608, 256)

    g1_next = send(own[1], "section", previous), send(other[1], "section", previous)
    g1_next = jnp.where(y == 0, g1_next[0], g1_next[1]), jnp.where(y == 0, g1_next[1], g1_next[0])
    which_next = send(assign, "section", previous)[0, 0]

    n2, unused = lax.optimization_barrier((scaled(next_batch, second_share), far_n[0]))
    found, far = ring(n2[None])
    routes = Routes()
    for offset, block in found.items():
        routes.add(block, [(0, None, offset, None)])
    for half in (0, 1):
        routes.add(far[half], [(0, None, 4, half)])
    (n2_plane,) = assemble(routes.arrays, routes.routes, [plane], place)
    n2_other = send(n2_plane, "tensor", SWAP_Y)
    n2_full = jnp.where(
        y == 0, jnp.stack([n2_plane, n2_other]), jnp.stack([n2_other, n2_plane])
    ).reshape(4608, 256)

    weights = jnp.concatenate([w_query, w_key, w_value], axis=1)
    saved1 = forward(n1_full, weights)
    proj1 = backward(saved1, g1_full, w_output)
    dn1 = mul(weights, proj1, ROW).astype(BF16).reshape(full)
    g2 = []
    routes = Routes()
    for chain in (0, 1):
        part1 = scatter_chain(dn1, chain, z).astype(BF16)
        here = send(part1, ("section", "tensor"), to_previous(0))
        there = send(part1, ("section", "tensor"), to_previous(8))
        branch = here.astype(F32) + there.astype(F32)
        scale = share(which_next, z + 8 * chain)
        shard = (g1_next[chain].astype(F32) + scale * branch).astype(BF16)
        g2.append(shard)
        found, far = ring(shard[None])
        for offset, block in found.items():
            routes.add(block, [(0, 2 + chain, offset, None)])
        for half in (0, 1):
            routes.add(far[half], [(0, 2 + chain, 4, half)])
    (g2_full,) = assemble(routes.arrays, routes.routes, [full], place)
    g2_full = g2_full.reshape(4608, 256)

    grads1 = jnp.concatenate([mul(n1_full, proj1, NT), mul(g1_full, saved1[4], NT)], axis=1)
    grads1 = lax.psum_scatter(grads1.astype(BF16), "section", scatter_dimension=0, tiled=True)

    saved2 = forward(n2_full, weights)
    proj2 = backward(saved2, g2_full, w_output)
    right2 = mul(g2_full, saved2[4], NT).astype(BF16).reshape(2, 4, 2, 288, 256)
    right2 = section_scatter(right2, core, x, yhi)

    dn2 = mul(weights, proj2, ROW).astype(BF16).reshape(full)
    part2 = [scatter_chain(dn2, chain, z) for chain in (0, 1)]
    away = jnp.where(y == 0, part2[1], part2[0]).astype(BF16)
    keep = jnp.where(y == 0, part2[0], part2[1])
    dn2_own = keep + send(away, "tensor", SWAP_Y).astype(F32)
    g2_own = jnp.where(y == 0, g2[0], g2[1])
    dx2 = (g2_own.astype(F32) + second_share * dn2_own).astype(BF16)

    left2 = mul(n2_full, proj2, NT).astype(BF16).reshape(2, 4, 2, 288, 512)
    left2 = section_scatter(left2, core, x, yhi)
    left = grads1[:, :512].astype(F32) + left2
    right = grads1[:, 512:].astype(F32) + right2
    return (
        dx2.T[None],
        left[:, :256],
        left[:, 256:384],
        left[:, 384:],
        right.T,
    )


def solution(mesh):
    in_specs = (
        P("section", None, None, "tensor"),
        P("section", None, "tensor"),
        P(),
        P("section", None),
        P(),
        P(None, "tensor"),
        P(None, "tensor"),
        P(None, "tensor"),
        P("tensor", None),
    )
    out_specs = (
        P("section", None, "tensor"),
        P("section", "tensor"),
        P("section", "tensor"),
        P("section", "tensor"),
        P("tensor", "section"),
    )
    return jax.shard_map(body, mesh=mesh, in_specs=in_specs, out_specs=out_specs, check_vma=False)
```

time: 599 us -> 613 us (1.023); the launches traced: 597 us -> 603 us
  waiting for transfers between devices: 478 us -> 41.8 us
  Pallas kernels: 0 us -> 256 us
  starting transfers between devices: 0.55 us -> 144 us
  local copies, waits for them, and re-layouts: 25.6 us -> 59.3 us
  other arithmetic: 15.2 us -> 44.3 us
  matrix products: 62.2 us -> 36.3 us
    all_gather x4 -> x0, waiting for transfers between devices: 258 us -> none  [the longest x1 72.9 us: body(): lax.all_gather(first_scaled, 'tensor', axis=1, tiled=True)]
    pallas_call x0 -> x3, Pallas kernels: none -> 256 us  [assemble(): pl.pallas_call(functools.partial(assemble_kernel, routes, len(arrays)), o...]
    ppermute x1 -> x98, starting transfers between devices: 0.08 us -> 144 us  [send(): return lax.ppermute(a, axis, pairs)]
    reduce_scatter x2 -> x0, waiting for transfers between devices: 116 us -> none  [the longest x1 71.9 us: body(): lax.psum_scatter(first_branch.astype(jnp.bfloat16), 'tensor', scatter_dim...]
    unnamed x8 -> x2, waiting for transfers between devices: 101 us -> 0.02 us
    ppermute x1 -> x98, waiting for transfers between devices: 2.67 us -> 41.8 us  [send(): return lax.ppermute(a, axis, pairs)]
    dot_general x26 -> x34, matrix products: 58.9 us -> 36.3 us  [mul(): return lax.dot_general(a, b, dims, preferred_element_type=F32)]
    add x0 -> x15, other arithmetic: none -> 17.4 us  [the longest x2 5.24 us: section_scatter(): both = side(core) + send(side(1 - core), 'section', SWAP_CORE)]
  transfers between devices with their start and end apart: 8 -> 99, of which waited for: 8 -> 22; matrix products, arithmetic and copies ran while one was open for 9% -> 20% of each run, Pallas kernels for 0% -> 18%
where the time goes in v1:
time: 613 us; the launch traced here: 603 us
  Pallas kernels  256 us (42%)
  starting transfers between devices  144 us (23%)
  local copies, waits for them, and re-layouts  59.3 us (10%)
  other arithmetic  44.3 us (7%)
  waiting for transfers between devices  41.8 us (7%)
  matrix products  36.3 us (6%)
  between operations  21 us (3%)
    pallas_call x3, Pallas kernels, assemble(): pl.pallas_call(functools.partial(assemble_kernel, routes, len(arrays)), o...  256 us
    ppermute x98, starting transfers between devices, send(): return lax.ppermute(a, axis, pairs)  144 us
    ppermute x98, waiting for transfers between devices, send(): return lax.ppermute(a, axis, pairs)  41.8 us
    dot_general x34, matrix products, mul(): return lax.dot_general(a, b, dims, preferred_element_type=F32)  36.3 us
    unnamed x133, local copies, waits for them, and re-layouts  22.8 us
  transfers between devices with their start and end apart: 99, of which 22 were waited for; matrix products, arithmetic and copies ran while one was open for 20% of the time, Pallas kernels for 18%

profile of v1, /device:TPU:8, one launch (start us, length us, event | category | flops | bytes accessed | tf_op | source)
XLA Modules:
  0.0 602.7 jit_solution(10082086632654983419)
XLA Ops:
  7.2 4.0 collective-permute-start.3
  24.1 2.0 collective-permute-start.4
  26.1 4.0 collective-permute-start.5
  31.5 3.7 collective-permute-done.4.refs_1_
  35.2 3.6 collective-permute-start.7
  38.8 3.3 constant_dynamic-update-slice_fusion.2
  42.8 3.2 collective-permute-start.13
  46.1 3.5 collective-permute-start.9
  51.7 2.0 collective-permute-start.20
  53.7 3.2 collective-permute-start.15
  57.2 3.6 collective-permute-start.11
  63.7 3.5 collective-permute-start.17
  72.3 3.3 collective-permute-start.19
  78.5 145.0 %shard_map.128 = (bf16[2,8,288,256]{3,2,1,0:T(8,128)(2,1)}, bf16[2,8,288,256]{3,2,1,0:T(8,128)(2,1)}) custom-call(s32[2]{0:T(128)} %pad_add_fusion.place_ref, bf16[2,288,256]{2,1,0:T(8,128)(2,1)} %copy-done.18, bf16[2,288,256]{2,1,0:T(8,128)(2,1)} %copy-done.26, bf16[2,288,256]{2,1,0:T(8,128)(2,1)} %copy-done.27, bf16[2,288,256]{2,1,0:T(8,128)(2,1)} %copy-done.28, ...), custom_call_target="tpu_custom_call" | custom-call | bytes 5000000 | tf_op jit(solution)/shard_map/pallas_call | solution.py:83
  223.6 4.7 convolution_convert_fusion.7
  231.6 3.8 convolution_convert_fusion.5
  239.1 2.0 collective-permute-start.24
  249.0 2.1 collective-permute-start.35
  261.1 1.9 collective-permute-start.47
  263.6 2.5 collective-permute-done.36
  266.2 2.1 bitcast_add_fusion.15
  272.3 2.4 collective-permute-start.49
  281.8 5.3 convolution_convert_fusion.1
  287.3 5.8 collective-permute-start.2
  293.2 3.2 collective-permute-start.51
  302.8 37.6 %shard_map.129 = bf16[8,288,256]{2,1,0:T(8,128)(2,1)} custom-call(s32[2]{0:T(128)} %pad_add_fusion.place_ref, bf16[1,288,256]{2,1,0:T(8,128)(2,1)} %bitcast.290, bf16[1,288,256]{2,1,0:T(8,128)(2,1)} %copy-done.38, bf16[1,288,256]{2,1,0:T(8,128)(2,1)} %collective-permute-done.45.refs_2_, bf16[1,288,256]{2,1,0:T(8,128)(2,1)} %collective-permute-done.46.refs_3_, ...), custom_call_target="tpu_custom_call" | custom-call | bytes 5000000 | tf_op jit(solution)/shard_map/pallas_call | solution.py:83
  342.6 3.4 collective-permute-start.54
  346.1 3.2 collective-permute-start.62
  350.5 3.2 collective-permute-start.56
  353.7 3.3 collective-permute-start.64
  358.0 3.4 collective-permute-start.58
  361.4 3.2 collective-permute-start.66
  364.7 5.6 pad_maximum_fusion
  370.3 10.3 %copy.40 = bf16[4608,768]{1,0:T(8,128)(2,1)} copy(bf16[4608,768]{0,1:T(8,128)(2,1)} %pad_maximum_fusion) | data formatting | bytes 14155776
  382.6 3.2 collective-permute-start.60
  387.6 3.7 collective-permute-start.68
  391.3 2.1 maximum_select_fusion
  393.4 5.0 convolution_convert_fusion.6
  400.7 73.4 %shard_map.130 = bf16[2,8,288,256]{3,2,1,0:T(8,128)(2,1)} custom-call(s32[2]{0:T(128)} %pad_add_fusion.place_ref, bf16[1,288,256]{2,1,0:T(8,128)(2,1)} %bitcast.289, bf16[1,288,256]{2,1,0:T(8,128)(2,1)} %copy-done.43, bf16[1,288,256]{2,1,0:T(8,128)(2,1)} %copy-done.44, bf16[1,288,256]{2,1,0:T(8,128)(2,1)} %collective-permute-done.55.refs_3_, ...), custom_call_target="tpu_custom_call" | custom-call | bytes 5000000 | tf_op jit(solution)/shard_map/pallas_call | solution.py:83
  474.1 2.5 fusion.6
  478.5 3.9 convolution_convert_fusion.4
  482.7 3.2 collective-permute-start.81
  485.9 1.9 collective-permute-start.73
  489.3 2.7 constant_dynamic-slice_fusion.1
  493.3 3.2 collective-permute-start.82
  496.6 2.1 collective-permute-start.70
  498.7 2.0 collective-permute-done.78
  503.8 3.6 collective-permute-done.79
  507.6 2.3 collective-permute-start.75
  509.9 3.7 collective-permute-done.83
  515.2 2.1 collective-permute-done.71
  521.7 2.8 copy.24
  526.1 2.0 select_convert_fusion
  529.1 2.6 copy.34
  531.6 2.1 bitcast_add_fusion.1
  534.6 3.2 collective-permute-start.93
  538.0 4.5 copy.25
  542.6 3.2 bitcast_add_fusion
  549.4 5.6 collective-permute-done.87
  561.2 2.1 fusion.37
  565.2 3.0 collective-permute-start.96
  569.0 3.4 collective-permute-done.90
  573.9 2.6 collective-permute-done.88
  586.3 2.5 collective-permute-done.91
  (400 shorter events, 124.2 us)
Async XLA Ops:
  7.2 577.9 %reduce-scatter.4.cloned.1.call-start = ((), (), s32[]{:S(2)}) async-start(), calls=%async_computation.1 | async-start | bytes 7520256
  7.2 13.4 %collective-permute-start.3 = (s32[1,2]{1,0:T(1,128)}, s32[1,2]{1,0:T(1,128)S(1)}, u32[]{:S(2)}, u32[]{:S(2)}) collective-permute-start(s32[1,2]{1,0:T(1,128)} %param.12), channel_id=1, source_target_pairs={{0,240},{16,0},{32,16},{48,32},{64,48},{80,64},{96,80},{112,96},{1... | collective-permute-start | bytes 32 | tf_op jit(solution)/shard_map/ppermute | solution.py:44
  24.1 11.0 %collective-permute-start.4 = (bf16[2,288,256]{2,1,0:T(8,128)(2,1)S(1)}, bf16[2,288,256]{2,1,0:T(8,128)(2,1)S(1)}, u32[]{:S(2)}, u32[]{:S(2)}) collective-permute-start(bf16[2,288,256]{2,1,0:T(8,128)(2,1)S(1)} %pad_maximum_fusion.5.refs_0_), channel_id=1, source_target_pairs={{0,1},{1,2},{2,3},{3,4},{4,5},{5,6},{6,7},{7,0},{8,9},{9,10},{10,1... | collective-permute-start | bytes 884744 | tf_op jit(solution)/shard_map/ppermute | solution.py:44
  26.1 9.1 %collective-permute-start.5 = (bf16[2,288,256]{2,1,0:T(8,128)(2,1)S(1)}, bf16[2,288,256]{2,1,0:T(8,128)(2,1)S(1)}, u32[]{:S(2)}, u32[]{:S(2)}) collective-permute-start(bf16[2,288,256]{2,1,0:T(8,128)(2,1)S(1)} %pad_maximum_fusion.5.refs_0_), channel_id=1, source_target_pairs={{0,7},{1,0},{2,1},{3,2},{4,3},{5,4},{6,5},{7,6},{8,15},{9,8},{10,9... | collective-permute-start | bytes 884744 | tf_op jit(solution)/shard_map/ppermute | solution.py:44
  30.1 12.0 %collective-permute-start.1 = (bf16[2,288,256]{2,1,0:T(8,128)(2,1)S(1)}, bf16[2,288,256]{2,1,0:T(8,128)(2,1)S(1)}, u32[]{:S(2)}, u32[]{:S(2)}) collective-permute-start(bf16[2,288,256]{2,1,0:T(8,128)(2,1)S(1)} %pad_maximum_fusion.5.refs_0_), channel_id=1, source_target_pairs={{0,8},{1,9},{2,10},{3,11},{4,12},{5,13},{6,14},{7,15},{8,0},{9,1},... | collective-permute-start | bytes 884744 | tf_op jit(solution)/shard_map/ppermute | solution.py:44
  35.2 10.9 %collective-permute-start.6 = (bf16[2,288,256]{2,1,0:T(8,128)(2,1)S(1)}, bf16[2,288,256]{2,1,0:T(8,128)(2,1)S(1)}, u32[]{:S(2)}, u32[]{:S(2)}) collective-permute-start(bf16[2,288,256]{2,1,0:T(8,128)(2,1)S(1)} %collective-permute-done.4.refs_1_), channel_id=1, source_target_pairs={{0,1},{1,2},{2,3},{3,4},{4,5},{5,6},{6,7},{7,0},{8,9},{9,10},{10,1... | collective-permute-start | bytes 884744 | tf_op jit(solution)/shard_map/ppermute | solution.py:44
  35.2 10.9 %collective-permute-start.7 = (bf16[2,288,256]{2,1,0:T(8,128)(2,1)S(1)}, bf16[2,288,256]{2,1,0:T(8,128)(2,1)S(1)}, u32[]{:S(2)}, u32[]{:S(2)}) collective-permute-start(bf16[2,288,256]{2,1,0:T(8,128)(2,1)S(1)} %collective-permute-done.5.refs_2_), channel_id=1, source_target_pairs={{0,7},{1,0},{2,1},{3,2},{4,3},{5,4},{6,5},{7,6},{8,15},{9,8},{10,9... | collective-permute-start | bytes 884744 | tf_op jit(solution)/shard_map/ppermute | solution.py:44
  42.8 10.9 %collective-permute-start.13 = (bf16[1,288,256]{2,1,0:T(8,128)(2,1)S(1)}, bf16[1,288,256]{2,1,0:T(8,128)(2,1)S(1)}, u32[]{:S(2)}, u32[]{:S(2)}) collective-permute-start(bf16[1,288,256]{2,1,0:T(8,128)(2,1)S(1)} %get-tuple-element.87), channel_id=1, source_target_pairs={{0,7},{1,0},{2,1},{3,2},{4,3},{5,4},{6,5},{7,6},{8,15},{9,8},{10,9... | collective-permute-start | bytes 442376 | tf_op jit(solution)/shard_map/ppermute | solution.py:44
  46.1 10.9 %collective-permute-start.8 = (bf16[2,288,256]{2,1,0:T(8,128)(2,1)S(1)}, bf16[2,288,256]{2,1,0:T(8,128)(2,1)S(1)}, u32[]{:S(2)}, u32[]{:S(2)}) collective-permute-start(bf16[2,288,256]{2,1,0:T(8,128)(2,1)S(1)} %collective-permute-done.6.refs_3_), channel_id=1, source_target_pairs={{0,1},{1,2},{2,3},{3,4},{4,5},{5,6},{6,7},{7,0},{8,9},{9,10},{10,1... | collective-permute-start | bytes 884744 | tf_op jit(solution)/shard_map/ppermute | solution.py:44
  46.1 11.0 %collective-permute-start.9 = (bf16[2,288,256]{2,1,0:T(8,128)(2,1)S(1)}, bf16[2,288,256]{2,1,0:T(8,128)(2,1)S(1)}, u32[]{:S(2)}, u32[]{:S(2)}) collective-permute-start(bf16[2,288,256]{2,1,0:T(8,128)(2,1)S(1)} %collective-permute-done.7.refs_4_), channel_id=1, source_target_pairs={{0,7},{1,0},{2,1},{3,2},{4,3},{5,4},{6,5},{7,6},{8,15},{9,8},{10,9... | collective-permute-start | bytes 884744 | tf_op jit(solution)/shard_map/ppermute | solution.py:44
  50.8 10.7 %collective-permute-start.14 = (bf16[1,288,256]{2,1,0:T(8,128)(2,1)S(1)}, bf16[1,288,256]{2,1,0:T(8,128)(2,1)S(1)}, u32[]{:S(2)}, u32[]{:S(2)}) collective-permute-start(bf16[1,288,256]{2,1,0:T(8,128)(2,1)S(1)} %collective-permute-done.12.refs_9_), channel_id=1, source_target_pairs={{0,1},{1,2},{2,3},{3,4},{4,5},{5,6},{6,7},{7,0},{8,9},{9,10},{10,1... | collective-permute-start | bytes 442376 | tf_op jit(solution)/shard_map/ppermute | solution.py:44
  51.7 20.6 %collective-permute-start.20 = (bf16[2,288,256]{2,1,0:T(8,128)(2,1)}, bf16[2,288,256]{2,1,0:T(8,128)(2,1)}, u32[]{:S(2)}, u32[]{:S(2)}) collective-permute-start(bf16[2,288,256]{2,1,0:T(8,128)(2,1)} %pad_maximum_fusion.6), channel_id=1, source_target_pairs={{0,8},{1,9},{2,10},{3,11},{4,12},{5,13},{6,14},{7,15},{8,0},{9,1},... | collective-permute-start | bytes 884744 | tf_op jit(solution)/shard_map/ppermute | solution.py:44
  53.7 8.6 %collective-permute-start.15 = (bf16[1,288,256]{2,1,0:T(8,128)(2,1)S(1)}, bf16[1,288,256]{2,1,0:T(8,128)(2,1)}, u32[]{:S(2)}, u32[]{:S(2)}) collective-permute-start(bf16[1,288,256]{2,1,0:T(8,128)(2,1)S(1)} %collective-permute-done.13.refs_10_), channel_id=1, source_target_pairs={{0,7},{1,0},{2,1},{3,2},{4,3},{5,4},{6,5},{7,6},{8,15},{9,8},{10,9... | collective-permute-start | bytes 442376 | tf_op jit(solution)/shard_map/ppermute | solution.py:44
  57.0 10.1 %collective-permute-start.10 = (bf16[2,144,256]{2,1,0:T(8,128)(2,1)S(1)}, bf16[2,144,256]{2,1,0:T(8,128)(2,1)S(1)}, u32[]{:S(2)}, u32[]{:S(2)}) collective-permute-start(bf16[2,144,256]{2,1,0:T(8,128)(2,1)S(1)} %slice.469), channel_id=1, source_target_pairs={{0,1},{1,2},{2,3},{3,4},{4,5},{5,6},{6,7},{7,0},{8,9},{9,10},{10,1... | collective-permute-start | bytes 442376 | tf_op jit(solution)/shard_map/ppermute | solution.py:44
  62.3 15.5 %collective-permute-start.21 = (bf16[2,288,256]{2,1,0:T(8,128)(2,1)}, bf16[2,288,256]{2,1,0:T(8,128)(2,1)}, u32[]{:S(2)}, u32[]{:S(2)}) collective-permute-start(bf16[2,288,256]{2,1,0:T(8,128)(2,1)} %pad_maximum_fusion.7), channel_id=1, source_target_pairs={{0,8},{1,9},{2,10},{3,11},{4,12},{5,13},{6,14},{7,15},{8,0},{9,1},... | collective-permute-start | bytes 884744 | tf_op jit(solution)/shard_map/ppermute | solution.py:44
  63.7 8.5 %collective-permute-start.17 = (bf16[1,288,256]{2,1,0:T(8,128)(2,1)}, bf16[1,288,256]{2,1,0:T(8,128)(2,1)S(1)}, u32[]{:S(2)}, u32[]{:S(2)}) collective-permute-start(bf16[1,288,256]{2,1,0:T(8,128)(2,1)} %collective-permute-done.15.refs_12_), channel_id=1, source_target_pairs={{0,7},{1,0},{2,1},{3,2},{4,3},{5,4},{6,5},{7,6},{8,15},{9,8},{10,9... | collective-permute-start | bytes 442376 | tf_op jit(solution)/shard_map/ppermute | solution.py:44
  67.2 10.7 %collective-permute-start.22 = (bf16[2,288,256]{2,1,0:T(8,128)(2,1)}, bf16[2,288,256]{2,1,0:T(8,128)(2,1)}, u32[]{:S(2)}, u32[]{:S(2)}) collective-permute-start(bf16[2,288,256]{2,1,0:T(8,128)(2,1)} %pad_maximum_fusion.8), channel_id=1, source_target_pairs={{0,8},{1,9},{2,10},{3,11},{4,12},{5,13},{6,14},{7,15},{8,0},{9,1},... | collective-permute-start | bytes 884744 | tf_op jit(solution)/shard_map/ppermute | solution.py:44
  69.3 8.5 %collective-permute-start.23 = (bf16[2,144,256]{2,1,0:T(8,128)(2,1)}, bf16[2,144,256]{2,1,0:T(8,128)(2,1)S(1)}, u32[]{:S(2)}, u32[]{:S(2)}) collective-permute-start(bf16[2,144,256]{2,1,0:T(8,128)(2,1)} %pad_maximum_fusion.11), channel_id=1, source_target_pairs={{0,8},{1,9},{2,10},{3,11},{4,12},{5,13},{6,14},{7,15},{8,0},{9,1},... | collective-permute-start | bytes 442376 | tf_op jit(solution)/shard_map/ppermute | solution.py:44
  243.2 14.8 %collective-permute-start.44 = (bf16[1,288,256]{2,1,0:T(8,128)(2,1)S(1)}, bf16[1,288,256]{2,1,0:T(8,128)(2,1)S(1)}, u32[]{:S(2)}, u32[]{:S(2)}) collective-permute-start(bf16[1,288,256]{2,1,0:T(8,128)(2,1)S(1)} %bitcast.291), channel_id=1, source_target_pairs={{0,1},{1,2},{2,3},{3,4},{4,5},{5,6},{6,7},{7,0},{8,9},{9,10},{10,1... | collective-permute-start | bytes 442376 | tf_op jit(solution)/shard_map/ppermute | solution.py:44
  244.6 15.2 %collective-permute-start.45 = (bf16[1,288,256]{2,1,0:T(8,128)(2,1)S(1)}, bf16[1,288,256]{2,1,0:T(8,128)(2,1)}, u32[]{:S(2)}, u32[]{:S(2)}) collective-permute-start(bf16[1,288,256]{2,1,0:T(8,128)(2,1)S(1)} %bitcast.292), channel_id=1, source_target_pairs={{0,7},{1,0},{2,1},{3,2},{4,3},{5,4},{6,5},{7,6},{8,15},{9,8},{10,9... | collective-permute-start | bytes 442376 | tf_op jit(solution)/shard_map/ppermute | solution.py:44
  251.8 9.3 %collective-permute-start.39 = (bf16[288,256]{1,0:T(8,128)(2,1)}, bf16[288,256]{1,0:T(8,128)(2,1)S(1)}, u32[]{:S(2)}, u32[]{:S(2)}) collective-permute-start(bf16[288,256]{1,0:T(8,128)(2,1)} %pad_maximum_fusion.15), channel_id=1, source_target_pairs={{0,7},{1,0},{2,1},{3,2},{4,3},{5,4},{6,5},{7,6},{8,15},{9,8},{10,9... | collective-permute-start | bytes 442376 | tf_op jit(solution)/shard_map/ppermute | solution.py:44
  253.7 9.3 %collective-permute-start.29 = (bf16[288,256]{1,0:T(8,128)(2,1)}, bf16[288,256]{1,0:T(8,128)(2,1)}, u32[]{:S(2)}, u32[]{:S(2)}) collective-permute-start(bf16[288,256]{1,0:T(8,128)(2,1)} %pad_maximum_fusion.13), channel_id=1, source_target_pairs={{0,7},{1,0},{2,1},{3,2},{4,3},{5,4},{6,5},{7,6},{8,15},{9,8},{10,9... | collective-permute-start | bytes 442376 | tf_op jit(solution)/shard_map/ppermute | solution.py:44
  255.5 8.2 %collective-permute-start.25 = (bf16[288,256]{1,0:T(8,128)(2,1)}, bf16[288,256]{1,0:T(8,128)(2,1)S(1)}, u32[]{:S(2)}, u32[]{:S(2)}) collective-permute-start(bf16[288,256]{1,0:T(8,128)(2,1)} %pad_maximum_fusion.12), channel_id=1, source_target_pairs={{0,1},{1,2},{2,3},{3,4},{4,5},{5,6},{6,7},{7,0},{8,9},{9,10},{10,1... | collective-permute-start | bytes 442376 | tf_op jit(solution)/shard_map/ppermute | solution.py:44
  259.8 11.7 %collective-permute-start.46 = (bf16[1,288,256]{2,1,0:T(8,128)(2,1)}, bf16[1,288,256]{2,1,0:T(8,128)(2,1)}, u32[]{:S(2)}, u32[]{:S(2)}) collective-permute-start(bf16[1,288,256]{2,1,0:T(8,128)(2,1)} %copy-done.38), channel_id=1, source_target_pairs={{0,1},{1,2},{2,3},{3,4},{4,5},{5,6},{6,7},{7,0},{8,9},{9,10},{10,1... | collective-permute-start | bytes 442376 | tf_op jit(solution)/shard_map/ppermute | solution.py:44
  261.1 11.2 %collective-permute-start.47 = (bf16[1,288,256]{2,1,0:T(8,128)(2,1)}, bf16[1,288,256]{2,1,0:T(8,128)(2,1)}, u32[]{:S(2)}, u32[]{:S(2)}) collective-permute-start(bf16[1,288,256]{2,1,0:T(8,128)(2,1)} %collective-permute-done.45.refs_2_), channel_id=1, source_target_pairs={{0,7},{1,0},{2,1},{3,2},{4,3},{5,4},{6,5},{7,6},{8,15},{9,8},{10,9... | collective-permute-start | bytes 442376 | tf_op jit(solution)/shard_map/ppermute | solution.py:44
  271.5 9.1 %collective-permute-start.48 = (bf16[1,288,256]{2,1,0:T(8,128)(2,1)}, bf16[1,288,256]{2,1,0:T(8,128)(2,1)S(1)}, u32[]{:S(2)}, u32[]{:S(2)}) collective-permute-start(bf16[1,288,256]{2,1,0:T(8,128)(2,1)} %collective-permute-done.46.refs_3_), channel_id=1, source_target_pairs={{0,1},{1,2},{2,3},{3,4},{4,5},{5,6},{6,7},{7,0},{8,9},{9,10},{10,1... | collective-permute-start | bytes 442376 | tf_op jit(solution)/shard_map/ppermute | solution.py:44
  272.3 14.9 %collective-permute-start.49 = (bf16[1,288,256]{2,1,0:T(8,128)(2,1)}, bf16[1,288,256]{2,1,0:T(8,128)(2,1)S(1)}, u32[]{:S(2)}, u32[]{:S(2)}) collective-permute-start(bf16[1,288,256]{2,1,0:T(8,128)(2,1)} %collective-permute-done.47.refs_4_), channel_id=1, source_target_pairs={{0,7},{1,0},{2,1},{3,2},{4,3},{5,4},{6,5},{7,6},{8,15},{9,8},{10,9... | collective-permute-start | bytes 442376 | tf_op jit(solution)/shard_map/ppermute | solution.py:44
  274.7 12.6 %collective-permute-start.37 = (bf16[288,256]{1,0:T(8,128)(2,1)S(1)}, bf16[288,256]{1,0:T(8,128)(2,1)S(1)}, u32[]{:S(2)}, u32[]{:S(2)}) collective-permute-start(bf16[288,256]{1,0:T(8,128)(2,1)S(1)} %get-tuple-element.55), channel_id=1, source_target_pairs={{0,1},{1,2},{2,3},{3,4},{4,5},{5,6},{6,7},{7,0},{8,9},{9,10},{10,1... | collective-permute-start | bytes 442376 | tf_op jit(solution)/shard_map/ppermute | solution.py:44
  277.9 15.2 %collective-permute-start.41 = (bf16[288,256]{1,0:T(8,128)(2,1)S(1)}, bf16[288,256]{1,0:T(8,128)(2,1)S(1)}, u32[]{:S(2)}, u32[]{:S(2)}) collective-permute-start(bf16[288,256]{1,0:T(8,128)(2,1)S(1)} %get-tuple-element.71), channel_id=1, source_target_pairs={{0,7},{1,0},{2,1},{3,2},{4,3},{5,4},{6,5},{7,6},{8,15},{9,8},{10,9... | collective-permute-start | bytes 442376 | tf_op jit(solution)/shard_map/ppermute | solution.py:44
  279.7 13.5 %collective-permute-start.31 = (bf16[288,256]{1,0:T(8,128)(2,1)S(1)}, bf16[288,256]{1,0:T(8,128)(2,1)S(1)}, u32[]{:S(2)}, u32[]{:S(2)}) collective-permute-start(bf16[288,256]{1,0:T(8,128)(2,1)S(1)} %get-tuple-element.72), channel_id=1, source_target_pairs={{0,7},{1,0},{2,1},{3,2},{4,3},{5,4},{6,5},{7,6},{8,15},{9,8},{10,9... | collective-permute-start | bytes 442376 | tf_op jit(solution)/shard_map/ppermute | solution.py:44
  280.6 15.8 %collective-permute-start.27 = (bf16[288,256]{1,0:T(8,128)(2,1)S(1)}, bf16[288,256]{1,0:T(8,128)(2,1)S(1)}, u32[]{:S(2)}, u32[]{:S(2)}) collective-permute-start(bf16[288,256]{1,0:T(8,128)(2,1)S(1)} %get-tuple-element.73), channel_id=1, source_target_pairs={{0,1},{1,2},{2,3},{3,4},{4,5},{5,6},{6,7},{7,0},{8,9},{9,10},{10,1... | collective-permute-start | bytes 442376 | tf_op jit(solution)/shard_map/ppermute | solution.py:44
  287.2 11.0 %collective-permute-start = (bf16[288,256]{1,0:T(8,128)(2,1)S(1)}, bf16[288,256]{1,0:T(8,128)(2,1)S(1)}, u32[]{:S(2)}, u32[]{:S(2)}) collective-permute-start(bf16[288,256]{1,0:T(8,128)(2,1)S(1)} %bitcast.294), channel_id=1, source_target_pairs={{0,240},{16,0},{32,16},{48,32},{64,48},{80,64},{96,80},{112,96},{1... | collective-permute-start | bytes 442376 | tf_op jit(solution)/shard_map/ppermute | solution.py:44
  287.3 53.1 %collective-permute-start.2 = (bf16[288,256]{1,0:T(8,128)(2,1)}, bf16[288,256]{1,0:T(8,128)(2,1)S(1)}, u32[]{:S(2)}, u32[]{:S(2)}) collective-permute-start(bf16[288,256]{1,0:T(8,128)(2,1)} %get-tuple-element.86), channel_id=1, source_target_pairs={{0,240},{16,0},{32,16},{48,32},{64,48},{80,64},{96,80},{112,96},{1... | collective-permute-start | bytes 442376 | tf_op jit(solution)/shard_map/ppermute | solution.py:44
  298.2 43.1 %collective-permute-start.43 = (bf16[288,256]{1,0:T(8,128)(2,1)}, bf16[288,256]{1,0:T(8,128)(2,1)S(1)}, u32[]{:S(2)}, u32[]{:S(2)}) collective-permute-start(bf16[288,256]{1,0:T(8,128)(2,1)} %get-tuple-element.53), channel_id=1, source_target_pairs={{0,248},{1,249},{2,250},{3,251},{4,252},{5,253},{6,254},{7,255},{8... | collective-permute-start | bytes 442376 | tf_op jit(solution)/shard_map/ppermute | solution.py:44
  298.2 43.1 %collective-permute-start.42 = (bf16[288,256]{1,0:T(8,128)(2,1)}, bf16[288,256]{1,0:T(8,128)(2,1)}, u32[]{:S(2)}, u32[]{:S(2)}) collective-permute-start(bf16[288,256]{1,0:T(8,128)(2,1)} %get-tuple-element.53), channel_id=1, source_target_pairs={{0,240},{1,241},{2,242},{3,243},{4,244},{5,245},{6,246},{7,247},{8... | collective-permute-start | bytes 442376 | tf_op jit(solution)/shard_map/ppermute | solution.py:44
  298.7 42.6 %collective-permute-start.33 = (bf16[288,256]{1,0:T(8,128)(2,1)}, bf16[288,256]{1,0:T(8,128)(2,1)}, u32[]{:S(2)}, u32[]{:S(2)}) collective-permute-start(bf16[288,256]{1,0:T(8,128)(2,1)} %get-tuple-element.54), channel_id=1, source_target_pairs={{0,248},{1,249},{2,250},{3,251},{4,252},{5,253},{6,254},{7,255},{8... | collective-permute-start | bytes 442376 | tf_op jit(solution)/shard_map/ppermute | solution.py:44
  299.4 41.9 %collective-permute-start.32 = (bf16[288,256]{1,0:T(8,128)(2,1)}, bf16[288,256]{1,0:T(8,128)(2,1)}, u32[]{:S(2)}, u32[]{:S(2)}) collective-permute-start(bf16[288,256]{1,0:T(8,128)(2,1)} %get-tuple-element.54), channel_id=1, source_target_pairs={{0,240},{1,241},{2,242},{3,243},{4,244},{5,245},{6,246},{7,247},{8... | collective-permute-start | bytes 442376 | tf_op jit(solution)/shard_map/ppermute | solution.py:44
  340.4 50.9 %collective-permute-start.52 = (bf16[8,288,256]{2,1,0:T(8,128)(2,1)}, bf16[8,288,256]{2,1,0:T(8,128)(2,1)}, u32[]{:S(2)}, u32[]{:S(2)}) collective-permute-start(bf16[8,288,256]{2,1,0:T(8,128)(2,1)} %shard_map.129), channel_id=1, source_target_pairs={{0,8},{1,9},{2,10},{3,11},{4,12},{5,13},{6,14},{7,15},{8,0},{9,1},... | collective-permute-start | bytes 3538952 | tf_op jit(solution)/shard_map/ppermute | solution.py:44
  358.0 22.7 %collective-permute-start.57 = (bf16[1,288,256]{2,1,0:T(8,128)(2,1)}, bf16[1,288,256]{2,1,0:T(8,128)(2,1)}, u32[]{:S(2)}, u32[]{:S(2)}) collective-permute-start(bf16[1,288,256]{2,1,0:T(8,128)(2,1)} %collective-permute-done.55.refs_3_), channel_id=1, source_target_pairs={{0,1},{1,2},{2,3},{3,4},{4,5},{5,6},{6,7},{7,0},{8,9},{9,10},{10,1... | collective-permute-start | bytes 442376 | tf_op jit(solution)/shard_map/ppermute | solution.py:44
  358.0 23.7 %collective-permute-start.58 = (bf16[1,288,256]{2,1,0:T(8,128)(2,1)}, bf16[1,288,256]{2,1,0:T(8,128)(2,1)}, u32[]{:S(2)}, u32[]{:S(2)}) collective-permute-start(bf16[1,288,256]{2,1,0:T(8,128)(2,1)} %collective-permute-done.56.refs_4_), channel_id=1, source_target_pairs={{0,7},{1,0},{2,1},{3,2},{4,3},{5,4},{6,5},{7,6},{8,15},{9,8},{10,9... | collective-permute-start | bytes 442376 | tf_op jit(solution)/shard_map/ppermute | solution.py:44
  361.4 24.4 %collective-permute-start.65 = (bf16[1,288,256]{2,1,0:T(8,128)(2,1)}, bf16[1,288,256]{2,1,0:T(8,128)(2,1)}, u32[]{:S(2)}, u32[]{:S(2)}) collective-permute-start(bf16[1,288,256]{2,1,0:T(8,128)(2,1)} %collective-permute-done.63.refs_12_), channel_id=1, source_target_pairs={{0,1},{1,2},{2,3},{3,4},{4,5},{5,6},{6,7},{7,0},{8,9},{9,10},{10,1... | collective-permute-start | bytes 442376 | tf_op jit(solution)/shard_map/ppermute | solution.py:44
  361.4 25.3 %collective-permute-start.66 = (bf16[1,288,256]{2,1,0:T(8,128)(2,1)}, bf16[1,288,256]{2,1,0:T(8,128)(2,1)}, u32[]{:S(2)}, u32[]{:S(2)}) collective-permute-start(bf16[1,288,256]{2,1,0:T(8,128)(2,1)} %collective-permute-done.64.refs_13_), channel_id=1, source_target_pairs={{0,7},{1,0},{2,1},{3,2},{4,3},{5,4},{6,5},{7,6},{8,15},{9,8},{10,9... | collective-permute-start | bytes 442376 | tf_op jit(solution)/shard_map/ppermute | solution.py:44
  381.7 17.8 %collective-permute-start.59 = (bf16[1,144,256]{2,1,0:T(8,128)(2,1)S(1)}, bf16[1,144,256]{2,1,0:T(8,128)(2,1)S(1)}, u32[]{:S(2)}, u32[]{:S(2)}) collective-permute-start(bf16[1,144,256]{2,1,0:T(8,128)(2,1)S(1)} %slice.493), channel_id=1, source_target_pairs={{0,1},{1,2},{2,3},{3,4},{4,5},{5,6},{6,7},{7,0},{8,9},{9,10},{10,1... | collective-permute-start | bytes 221192 | tf_op jit(solution)/shard_map/ppermute | solution.py:44
  382.6 16.9 %collective-permute-start.60 = (bf16[1,144,256]{2,1,0:T(8,128)(2,1)S(1)}, bf16[1,144,256]{2,1,0:T(8,128)(2,1)S(1)}, u32[]{:S(2)}, u32[]{:S(2)}) collective-permute-start(bf16[1,144,256]{2,1,0:T(8,128)(2,1)S(1)} %slice.494), channel_id=1, source_target_pairs={{0,7},{1,0},{2,1},{3,2},{4,3},{5,4},{6,5},{7,6},{8,15},{9,8},{10,9... | collective-permute-start | bytes 221192 | tf_op jit(solution)/shard_map/ppermute | solution.py:44
  386.7 12.8 %collective-permute-start.67 = (bf16[1,144,256]{2,1,0:T(8,128)(2,1)S(1)}, bf16[1,144,256]{2,1,0:T(8,128)(2,1)S(1)}, u32[]{:S(2)}, u32[]{:S(2)}) collective-permute-start(bf16[1,144,256]{2,1,0:T(8,128)(2,1)S(1)} %slice.495), channel_id=1, source_target_pairs={{0,1},{1,2},{2,3},{3,4},{4,5},{5,6},{6,7},{7,0},{8,9},{9,10},{10,1... | collective-permute-start | bytes 221192 | tf_op jit(solution)/shard_map/ppermute | solution.py:44
  387.6 13.1 %collective-permute-start.68 = (bf16[1,144,256]{2,1,0:T(8,128)(2,1)S(1)}, bf16[1,144,256]{2,1,0:T(8,128)(2,1)}, u32[]{:S(2)}, u32[]{:S(2)}) collective-permute-start(bf16[1,144,256]{2,1,0:T(8,128)(2,1)S(1)} %slice.496), channel_id=1, source_target_pairs={{0,7},{1,0},{2,1},{3,2},{4,3},{5,4},{6,5},{7,6},{8,15},{9,8},{10,9... | collective-permute-start | bytes 221192 | tf_op jit(solution)/shard_map/ppermute | solution.py:44
  482.5 10.3 %collective-permute-start.77 = (bf16[144,256]{1,0:T(8,128)(2,1)S(1)}, bf16[144,256]{1,0:T(8,128)(2,1)S(1)}, u32[]{:S(2)}, u32[]{:S(2)}) collective-permute-start(bf16[144,256]{1,0:T(8,128)(2,1)S(1)} %get-tuple-element.42), channel_id=1, source_target_pairs={{0,1},{1,2},{2,3},{3,4},{4,5},{5,6},{6,7},{7,0},{8,9},{9,10},{10,1... | collective-permute-start | bytes 221192 | tf_op jit(solution)/shard_map/ppermute | solution.py:44
  482.6 10.2 %collective-permute-start.69 = (bf16[144,256]{1,0:T(8,128)(2,1)S(1)}, bf16[144,256]{1,0:T(8,128)(2,1)S(1)}, u32[]{:S(2)}, u32[]{:S(2)}) collective-permute-start(bf16[144,256]{1,0:T(8,128)(2,1)S(1)} %get-tuple-element.45), channel_id=1, source_target_pairs={{0,1},{1,2},{2,3},{3,4},{4,5},{5,6},{6,7},{7,0},{8,9},{9,10},{10,1... | collective-permute-start | bytes 221192 | tf_op jit(solution)/shard_map/ppermute | solution.py:44
  482.7 10.1 %collective-permute-start.81 = (bf16[144,256]{1,0:T(8,128)(2,1)S(1)}, bf16[144,256]{1,0:T(8,128)(2,1)S(1)}, u32[]{:S(2)}, u32[]{:S(2)}) collective-permute-start(bf16[144,256]{1,0:T(8,128)(2,1)S(1)} %get-tuple-element.46), channel_id=1, source_target_pairs={{0,7},{1,0},{2,1},{3,2},{4,3},{5,4},{6,5},{7,6},{8,15},{9,8},{10,9... | collective-permute-start | bytes 221192 | tf_op jit(solution)/shard_map/ppermute | solution.py:44
  492.0 46.1 %collective-permute-start.86 = (bf16[2,4,288,512]{3,2,1,0:T(8,128)(2,1)}, bf16[2,4,288,512]{3,2,1,0:T(8,128)(2,1)}, u32[]{:S(2)}, u32[]{:S(2)}) collective-permute-start(bf16[2,4,288,512]{3,2,1,0:T(8,128)(2,1)} %get-tuple-element.26), channel_id=1, source_target_pairs={{0,16},{16,0},{32,48},{48,32},{64,80},{80,64},{96,112},{112,96},{1... | collective-permute-start | bytes 7077896 | tf_op jit(solution)/shard_map/ppermute | solution.py:44
  493.3 8.9 %collective-permute-start.82 = (bf16[288,256]{1,0:T(8,128)(2,1)S(1)}, bf16[288,256]{1,0:T(8,128)(2,1)S(1)}, u32[]{:S(2)}, u32[]{:S(2)}) collective-permute-start(bf16[288,256]{1,0:T(8,128)(2,1)S(1)} %pad_maximum_fusion.19), channel_id=1, source_target_pairs={{0,7},{1,0},{2,1},{3,2},{4,3},{5,4},{6,5},{7,6},{8,15},{9,8},{10,9... | collective-permute-start | bytes 442376 | tf_op jit(solution)/shard_map/ppermute | solution.py:44
  502.2 26.9 %collective-permute-start.92 = (bf16[2,4,288,256]{3,2,1,0:T(8,128)(2,1)}, bf16[2,4,288,256]{3,2,1,0:T(8,128)(2,1)}, u32[]{:S(2)}, u32[]{:S(2)}) collective-permute-start(bf16[2,4,288,256]{3,2,1,0:T(8,128)(2,1)} %get-tuple-element.33), channel_id=1, source_target_pairs={{0,16},{16,0},{32,48},{48,32},{64,80},{80,64},{96,112},{112,96},{1... | collective-permute-start | bytes 3538952 | tf_op jit(solution)/shard_map/ppermute | solution.py:44
  518.0 8.1 %collective-permute-start.76 = (bf16[288,256]{1,0:T(8,128)(2,1)}, bf16[288,256]{1,0:T(8,128)(2,1)}, u32[]{:S(2)}, u32[]{:S(2)}) collective-permute-start(bf16[288,256]{1,0:T(8,128)(2,1)} %get-tuple-element.51), channel_id=1, source_target_pairs={{0,7},{1,0},{2,1},{3,2},{4,3},{5,4},{6,5},{7,6},{8,15},{9,8},{10,9... | collective-permute-start | bytes 442376 | tf_op jit(solution)/shard_map/ppermute | solution.py:44
  528.1 33.0 %collective-permute-start.85 = (bf16[288,256]{1,0:T(8,128)(2,1)}, bf16[288,256]{1,0:T(8,128)(2,1)}, u32[]{:S(2)}, u32[]{:S(2)}) collective-permute-start(bf16[288,256]{1,0:T(8,128)(2,1)} %select_convert_fusion), channel_id=1, source_target_pairs={{0,8},{1,9},{2,10},{3,11},{4,12},{5,13},{6,14},{7,15},{8,0},{9,1},... | collective-permute-start | bytes 442376 | tf_op jit(solution)/shard_map/ppermute | solution.py:44
  534.6 28.7 %collective-permute-start.93 = (bf16[1,288,256]{1,2,0:T(8,128)(2,1)}, bf16[1,288,256]{1,2,0:T(8,128)(2,1)}, u32[]{:S(2)}, u32[]{:S(2)}) collective-permute-start(bf16[1,288,256]{1,2,0:T(8,128)(2,1)} %get-tuple-element.76), channel_id=1, source_target_pairs={{0,32},{16,48},{32,64},{48,80},{64,96},{80,112},{96,0},{112,16},{1... | collective-permute-start | bytes 442376 | tf_op jit(solution)/shard_map/ppermute | solution.py:44
  537.8 25.6 %collective-permute-start.95 = (bf16[1,288,256]{1,2,0:T(8,128)(2,1)}, bf16[1,288,256]{1,2,0:T(8,128)(2,1)}, u32[]{:S(2)}, u32[]{:S(2)}) collective-permute-start(bf16[1,288,256]{1,2,0:T(8,128)(2,1)} %get-tuple-element.78), channel_id=1, source_target_pairs={{0,96},{16,112},{32,0},{48,16},{64,32},{80,48},{96,64},{112,80},{1... | collective-permute-start | bytes 442376 | tf_op jit(solution)/shard_map/ppermute | solution.py:44
  545.9 9.1 %collective-permute-start.87 = (bf16[1,288,512]{1,2,0:T(8,128)(2,1)S(1)}, bf16[1,288,512]{1,2,0:T(8,128)(2,1)S(1)}, u32[]{:S(2)}, u32[]{:S(2)}) collective-permute-start(bf16[1,288,512]{1,2,0:T(8,128)(2,1)S(1)} %get-tuple-element.29), channel_id=1, source_target_pairs={{0,32},{16,48},{32,64},{48,80},{64,96},{80,112},{96,0},{112,16},{1... | collective-permute-start | bytes 884744 | tf_op jit(solution)/shard_map/ppermute | solution.py:44
  547.7 8.7 %collective-permute-start.89 = (bf16[1,288,512]{1,2,0:T(8,128)(2,1)S(1)}, bf16[1,288,512]{1,2,0:T(8,128)(2,1)S(1)}, u32[]{:S(2)}, u32[]{:S(2)}) collective-permute-start(bf16[1,288,512]{1,2,0:T(8,128)(2,1)S(1)} %get-tuple-element.31), channel_id=1, source_target_pairs={{0,96},{16,112},{32,0},{48,16},{64,32},{80,48},{96,64},{112,80},{1... | collective-permute-start | bytes 884744 | tf_op jit(solution)/shard_map/ppermute | solution.py:44
  557.8 14.6 %collective-permute-start.90 = (bf16[2,288,512]{2,1,0:T(8,128)(2,1)}, bf16[2,288,512]{2,1,0:T(8,128)(2,1)}, u32[]{:S(2)}, u32[]{:S(2)}) collective-permute-start(bf16[2,288,512]{2,1,0:T(8,128)(2,1)} %copy.31), channel_id=1, source_target_pairs={{0,96},{16,112},{32,0},{48,16},{64,32},{80,48},{96,64},{112,80},{1... | collective-permute-start | bytes 1769480 | tf_op jit(solution)/shard_map/ppermute | solution.py:44
  560.9 15.6 %collective-permute-start.88 = (bf16[2,288,512]{2,1,0:T(8,128)(2,1)}, bf16[2,288,512]{2,1,0:T(8,128)(2,1)}, u32[]{:S(2)}, u32[]{:S(2)}) collective-permute-start(bf16[2,288,512]{2,1,0:T(8,128)(2,1)} %copy.28), channel_id=1, source_target_pairs={{0,32},{16,48},{32,64},{48,80},{64,96},{80,112},{96,0},{112,16},{1... | collective-permute-start | bytes 1769480 | tf_op jit(solution)/shard_map/ppermute | solution.py:44
  565.2 16.0 %collective-permute-start.96 = (bf16[2,288,256]{1,2,0:T(8,128)(2,1)}, bf16[2,288,256]{1,2,0:T(8,128)(2,1)}, u32[]{:S(2)}, u32[]{:S(2)}) collective-permute-start(bf16[2,288,256]{1,2,0:T(8,128)(2,1)} %pad_maximum_fusion.4), channel_id=1, source_target_pairs={{0,96},{16,112},{32,0},{48,16},{64,32},{80,48},{96,64},{112,80},{1... | collective-permute-start | bytes 884744 | tf_op jit(solution)/shard_map/ppermute | solution.py:44
  569.0 12.2 %collective-permute-start.94 = (bf16[2,288,256]{1,2,0:T(8,128)(2,1)}, bf16[2,288,256]{1,2,0:T(8,128)(2,1)}, u32[]{:S(2)}, u32[]{:S(2)}) collective-permute-start(bf16[2,288,256]{1,2,0:T(8,128)(2,1)} %pad_maximum_fusion.3), channel_id=1, source_target_pairs={{0,32},{16,48},{32,64},{48,80},{64,96},{80,112},{96,0},{112,16},{1... | collective-permute-start | bytes 884744 | tf_op jit(solution)/shard_map/ppermute | solution.py:44
  579.4 9.4 %collective-permute-start.91 = (bf16[288,512]{0,1:T(8,128)(2,1)S(1)}, bf16[288,512]{0,1:T(8,128)(2,1)S(1)}, u32[]{:S(2)}, u32[]{:S(2)}) collective-permute-start(bf16[288,512]{0,1:T(8,128)(2,1)S(1)} %fusion.13), channel_id=1, source_target_pairs={{0,128},{16,144},{32,160},{48,176},{64,192},{80,208},{96,224},{112... | collective-permute-start | bytes 884744 | tf_op jit(solution)/shard_map/ppermute | solution.py:44
  583.3 10.3 %collective-permute-start.97 = (bf16[288,256]{0,1:T(8,128)(2,1)}, bf16[288,256]{0,1:T(8,128)(2,1)}, u32[]{:S(2)}, u32[]{:S(2)}) collective-permute-start(bf16[288,256]{0,1:T(8,128)(2,1)} %fusion.34), channel_id=1, source_target_pairs={{0,128},{16,144},{32,160},{48,176},{64,192},{80,208},{96,224},{112... | collective-permute-start | bytes 442376 | tf_op jit(solution)/shard_map/ppermute | solution.py:44
  (97 other events, 1018.0 us)
Sparse Core Ops, SparseCore 0:
  380.8 99.1 reduce-scatter.3
